TPU v7x, 32 devices: a whole 2x2x4 slice. The times are simulated.
32 devices in a mesh: dp: 2 (over y), seq: 16 (over z, x, core).
Axes of the slice: x: 2, y: 2, z: 4, core: 2. Of those that a mesh axis runs over, the one named last changes fastest.
Arguments:
- hidden_in: bfloat16 [8, 4096, 768], P('dp', 'seq'), may hold values from -6 to 6
- positions: int32 [8, 4096], P('dp', 'seq'), may hold values from 0 to 4095
- ln1_gain: float32 [768], replicated, may hold values from 0.5 to 1.5
- ln1_bias: float32 [768], replicated, may hold values from -4 to 4
- ln2_gain: float32 [768], replicated, may hold values from 0.5 to 1.5
- ln2_bias: float32 [768], replicated, may hold values from -4 to 4
- query_projection: bfloat16 [768, 768], replicated, may hold values from -0.3125 to 0.3125
- query_bias: float32 [768], replicated, may hold values from -4 to 4
- shared_key_weight: bfloat16 [768, 64], replicated, may hold values from -0.21875 to 0.21875
- shared_key_bias: float32 [64], replicated, may hold values from -4 to 4
- shared_value_weight: bfloat16 [768, 64], replicated, may hold values from -0.21875 to 0.21875
- shared_value_bias: float32 [64], replicated, may hold values from -4 to 4
- output_weight: bfloat16 [768, 768], replicated, may hold values from -0.625 to 0.625
- output_bias: float32 [768], replicated, may hold values from -4 to 4
- up_weight: bfloat16 [768, 3072], replicated, may hold values from -0.21875 to 0.21875
- up_bias: float32 [3072], replicated, may hold values from -4 to 4
- down_weight: bfloat16 [3072, 768], replicated, may hold values from -0.109375 to 0.109375
- down_bias: float32 [768], replicated, may hold values from -4 to 4
- cotangent: bfloat16 [8, 4096, 768], P('dp', 'seq'), may hold values from -6 to 6
Outputs:
- layer_out: float32 [8, 4096, 768], P('dp', 'seq')
- input_grad: float32 [8, 4096, 768], P('dp', 'seq')
- grad_ln1_gain: float32 [768], replicated
- grad_ln1_bias: float32 [768], replicated
- grad_ln2_gain: float32 [768], replicated
- grad_ln2_bias: float32 [768], replicated
- grad_w_query: float32 [768, 768], replicated
- grad_b_query: float32 [768], replicated
- grad_w_key: float32 [768, 64], replicated
- grad_b_key: float32 [64], replicated
- grad_w_value: float32 [768, 64], replicated
- grad_b_value: float32 [64], replicated
- grad_w_out: float32 [768, 768], replicated
- grad_b_out: float32 [768], replicated
- up_weight_gradient: float32 [768, 3072], replicated
- grad_b_up: float32 [3072], replicated
- grad_w_down: float32 [3072, 768], replicated
- grad_b_down: float32 [768], replicated
All inputs are finite; a program needn't handle non-finite values.
Results may differ from a plain program's by a relative error of at most 0.033.
Values may be sent and summed in bfloat16 or wider, within the bound.
A program may use at most 192 MiB of HBM per device.

v0:
```python
import functools
import math

import jax
import jax.numpy as jnp
from jax import lax
from jax.experimental import pallas as pl
from jax.experimental.pallas import tpu as pltpu
from jax.sharding import PartitionSpec as P

D = 768
HEADS = 12
HEAD_DIM = 64
ROT_DIMS = 16
BF = jnp.bfloat16
F32 = jnp.float32
LOG2E = math.log2(math.e)


def layer_norm(values, gain, bias):
    center = values - jnp.mean(values, axis=-1, keepdims=True)
    spread = jnp.mean(center * center, axis=-1, keepdims=True)
    return center * lax.rsqrt(spread + 1e-05) * gain + bias


def rotary_rows(values, cosine, sine):
    half = cosine.shape[-2]
    first, second = values[..., :half, :], values[..., half : 2 * half, :]
    return jnp.concatenate(
        [first * cosine - second * sine, second * cosine + first * sine, values[..., 2 * half :, :]],
        axis=-2,
    )


def angles_of(positions):
    half = ROT_DIMS // 2
    frequency = jnp.exp(
        jnp.arange(half).astype(F32) * (-2.0 * math.log(10000.0) / ROT_DIMS)
    )
    angle = positions.astype(F32)[:, None, :] * frequency[None, :, None]
    return jnp.cos(angle), jnp.sin(angle)


MESH = pl.DeviceIdType.MESH


def dot(a, b, ca, cb):
    return lax.dot_general(a, b, (((ca,), (cb,)), ((), ())), preferred_element_type=F32)


def flip(index, weight):
    return index + weight - 2 * weight * lax.rem(index // weight, 2)


def gelu_parts(u):
    e = jnp.exp(u * u * -0.5)
    t = 1.0 / (1.0 + (0.3275911 / math.sqrt(2.0)) * jnp.abs(u))
    poly = t * (
        0.5 * 0.254829592
        + t
        * (
            0.5 * -0.284496736
            + t * (0.5 * 1.421413741 + t * (0.5 * -1.453152027 + t * (0.5 * 1.061405429)))
        )
    )
    tail = poly * e
    return jnp.where(u >= 0, 1.0 - tail, tail), e * (1.0 / math.sqrt(2.0 * math.pi))


def feed_kernel(
    x_ref,
    c_ref,
    up_ref,
    down_ref,
    bias_ref,
    ff_ref,
    gx_ref,
    gup_ref,
    gdown_ref,
    gbias_ref,
    act_ref,
    grad_ref,
):
    tokens = x_ref.shape[0]
    bias = bias_ref[...]
    sub = min(256, tokens)
    for r in range(0, tokens, sub):
        u = dot(x_ref[r : r + sub, :], up_ref[...], 1, 0) + bias
        share, density = gelu_parts(u)
        act_ref[r : r + sub, :] = (u * share).astype(BF)
        da = dot(c_ref[r : r + sub, :], down_ref[...], 1, 1)
        grad_ref[r : r + sub, :] = (da * (share + u * density)).astype(BF)

    @pl.when(pl.program_id(0) == 0)
    def _():
        ff_ref[...] = jnp.zeros_like(ff_ref)
        gx_ref[...] = jnp.zeros_like(gx_ref)

    act, grad = act_ref[...], grad_ref[...]
    ff_ref[...] += dot(act, down_ref[...], 1, 0)
    gx_ref[...] += dot(grad, up_ref[...], 1, 1)
    gdown_ref[...] = dot(act, c_ref[...], 0, 0).astype(BF)
    gup_ref[...] = dot(x_ref[...], grad, 0, 0).astype(BF)
    gbias_ref[...] = jnp.sum(grad.astype(F32), axis=0, keepdims=True)


def feed_forward(x, cot, up_weight, up_bias, down_weight):
    tokens, d = x.shape
    ff = up_weight.shape[1]
    wide = d
    steps = ff // wide
    whole = pl.BlockSpec((tokens, d), lambda i: (0, 0))
    by_column = pl.BlockSpec((d, wide), lambda i: (0, i))
    by_row = pl.BlockSpec((wide, d), lambda i: (i, 0))
    line = pl.BlockSpec((1, wide), lambda i: (0, i))
    return pl.pallas_call(
        feed_kernel,
        grid=(steps,),
        out_shape=[
            jax.ShapeDtypeStruct((tokens, d), F32),
            jax.ShapeDtypeStruct((tokens, d), F32),
            jax.ShapeDtypeStruct((ff, d), BF),
            jax.ShapeDtypeStruct((ff, d), BF),
            jax.ShapeDtypeStruct((1, ff), F32),
        ],
        in_specs=[whole, whole, by_column, by_row, line],
        out_specs=[whole, whole, pl.BlockSpec((d, wide), lambda i: (i, 0)), by_row, line],
        scratch_shapes=[pltpu.VMEM((tokens, wide), BF), pltpu.VMEM((tokens, wide), BF)],
        compiler_params=pltpu.CompilerParams(vmem_limit_bytes=56 * 2**20),
        cost_estimate=pl.CostEstimate(
            flops=12 * tokens * d * ff,
            bytes_accessed=16 * d * ff,
            transcendentals=tokens * ff,
        ),
        name="feed_forward",
    )(x, cot, up_weight, down_weight, up_bias)


KEYS = 256


def shipped(upper_index, ring, tiles):
    more = upper_index + 2
    return (tiles * (2 * upper_index + 1 - ring) + more) // (2 * more)


class Exchange:
    def __init__(self, index, order, array, out, acc, recv, first, wide, sems):
        self.index, self.order, self.sems = index, order, sems
        self.array, self.out, self.acc, self.recv = array, out, acc, recv
        self.columns = pl.ds(first, wide)
        self.rows = array.shape[0]
        self.halvings = halvings_of(self.rows, len(order))
        self.waits = len(order)

    def size(self, s):
        return self.rows >> min(s, self.halvings)

    def base(self, s):
        return sum(self.size(t + 1) for t in range(s))

    def start(self, s, first=1):
        at = 0
        for t in range(first, min(s, self.halvings)):
            at = at + side_of(self.order[t]) * self.size(t + 1)
        return at

    def copy(self, k):
        bit = self.order[k]
        size = self.size(k + 1)
        other = self.start(k) + ((1 - side_of(bit)) * size if k < self.halvings else 0)
        rows = pl.ds(pl.multiple_of(other, size), size)
        src = (self.array if k == 0 else self.acc).at[rows, self.columns]
        dst = self.recv.at[pl.ds(self.base(k), size), self.columns]
        return pltpu.make_async_remote_copy(
            src_ref=src,
            dst_ref=dst,
            send_sem=self.sems[0].at[self.index, k],
            recv_sem=self.sems[1].at[self.index, k],
            device_id=partner_of(bit),
            device_id_type=MESH,
        )

    def fill(self):
        half = self.size(1)
        rows = pl.ds(pl.multiple_of(side_of(self.order[0]) * half, half), half)
        return pltpu.make_async_copy(
            self.array.at[rows, self.columns],
            self.acc.at[:, self.columns],
            self.sems[2].at[self.index],
        )

    def empty(self):
        size = self.size(self.halvings)
        rows = pl.ds(pl.multiple_of(self.start(self.halvings), size), size)
        return pltpu.make_async_copy(
            self.acc.at[rows, self.columns],
            self.out.at[:, self.columns],
            self.sems[3].at[self.index],
        )

    def begin(self):
        self.fill().start()
        self.copy(0).start()

    def take(self, k):
        self.copy(k).wait()
        if k == 0:
            self.fill().wait()
        size = self.size(k + 1)
        start = self.start(k + 1)
        step = next(n for n in (128, 96, 64, 48, 32, 16) if size % n == 0)
        base = self.base(k)

        def add(i, carry):
            r = pl.multiple_of(i * step, step)
            mine = pl.ds(pl.multiple_of(start + r, step), step)
            self.acc[mine, self.columns] = (
                self.acc[mine, self.columns] + self.recv[pl.ds(base + r, step), self.columns]
            )
            return carry

        lax.fori_loop(0, size // step, add, 0)
        if k == len(self.order) - 1:
            self.empty().start()
            self.empty().wait()
        if k + 1 < self.waits:
            self.copy(k + 1).start()


def owners(rows, order, dp, ring):
    halved = order[: halvings_of(rows, len(order))]
    found = []
    for segment in range(1 << len(halved)):
        place = {"dp": 0, "seq": 0}
        for t, (axis, weight) in enumerate(halved):
            place[axis] += weight * (segment >> (len(halved) - 1 - t) & 1)
        found.append(place["dp"] * ring + place["seq"])
    return found


def unpack_kernel(froms, all_ref, down_out, up_out, low, wide, come_sem, sent_sem):
    count = len(froms[0])
    tall, across = all_ref.shape[2:]
    come = [
        [
            pltpu.make_async_copy(all_ref.at[d, a], low.at[a, i], come_sem.at[a, i])
            for i, d in enumerate(froms[a])
        ]
        for a in range(2)
    ]
    for copy in come[0] + come[1]:
        copy.start()
    gone = []
    for a in range(2):
        for i in range(count):
            come[a][i].wait()
            wide[a, i] = low[a, i].astype(F32)
            at = i * tall
            if a == 0:
                to = down_out.at[pl.ds(at, tall), :]
            else:
                block = at // across
                to = up_out.at[pl.ds(at - block * across, tall), pl.ds(block * across, across)]
            gone.append(pltpu.make_async_copy(wide.at[a, i], to, sent_sem.at[a, i]))
            gone[-1].start()
    for copy in gone:
        copy.wait()


def unpack(parts, down_shape, up_shape, orders, dp, ring):
    everyone = lax.all_gather(parts, ("dp", "seq"))
    froms = [owners(down_shape[0], order, dp, ring) for order in orders]
    anywhere = pl.BlockSpec(memory_space=pl.ANY)
    dma = pltpu.SemaphoreType.DMA
    size = down_shape[0] * down_shape[1]
    count = len(froms[0])
    return pl.pallas_call(
        functools.partial(unpack_kernel, froms),
        out_shape=[jax.ShapeDtypeStruct(down_shape, F32), jax.ShapeDtypeStruct(up_shape, F32)],
        in_specs=[anywhere],
        out_specs=[anywhere] * 2,
        scratch_shapes=[
            pltpu.VMEM((2, count) + parts.shape[1:], BF),
            pltpu.VMEM((2, count) + parts.shape[1:], F32),
            dma((2, count)),
            dma((2, count)),
        ],
        compiler_params=pltpu.CompilerParams(vmem_limit_bytes=48 * 2**20),
        cost_estimate=pl.CostEstimate(flops=4 * size, bytes_accessed=12 * size, transcendentals=0),
        name="unpack",
    )(everyone)


def halvings_of(rows, stages):
    count = 0
    while count < stages and rows % (32 << count) == 0:
        count += 1
    return count


def exchange_rows(rows, stages):
    count = halvings_of(rows, stages)
    return sum(rows >> min(s + 1, count) for s in range(stages))


def attention_kernel(
    seqs,
    groups,
    orders,
    q_ref,
    g_ref,
    all_ref,
    down_ref,
    up_ref,
    att_ref,
    dq_ref,
    slot_ref,
    sum_ref,
    kvt_ref,
    flat_ref,
    rows_ref,
    dkv_ref,
    s_ref,
    p_ref,
    qs_ref,
    gs_ref,
    qin_ref,
    gin_ref,
    atts_ref,
    dqs_ref,
    stage_ref,
    half_ref,
    load_sem,
    own_sem,
    in_send,
    in_recv,
    out_send,
    out_recv,
    core_send,
    core_recv,
    slot_send,
    slot_recv,
    down_acc_ref,
    up_acc_ref,
    down_recv_ref,
    up_recv_ref,
    graw_ref,
    sum_send,
    sum_recv,
    fill_sem,
    empty_sem,
):
    tiles, width, rows = q_ref.shape
    ring = all_ref.shape[0]
    chips = ring // 2
    heads = width // HEAD_DIM
    lanes = heads * rows
    length = ring * rows
    me = lax.axis_index("seq")
    chip, core = me // 2, lax.rem(me, 2)
    upper = me // chips
    partner = ring - 1 - me
    count = shipped(me + (1 - upper) * (partner - me), ring, tiles)

    def to(index):
        return {"seq": index}

    barrier = pltpu.get_barrier_semaphore()

    def greet(index):
        pl.semaphore_signal(barrier, inc=1, device_id=to(index), device_id_type=MESH)

    greet(partner)
    greet(flip(me, 1))
    for m in range(1, chips):
        greet(lax.rem(me + 2 * m, ring))
    across = [bit for bit in orders[0] if bit[0] == "dp"]
    for bit in across:
        pl.semaphore_signal(
            barrier, inc=1, device_id=partner_of(bit), device_id_type=MESH
        )
    pl.semaphore_wait(barrier, chips + 1 + len(across))

    def load(s, slot):
        return pltpu.make_async_copy(
            all_ref.at[:, pl.ds(pl.multiple_of(s * 2 * HEAD_DIM, 2 * HEAD_DIM), 2 * HEAD_DIM), :],
            kvt_ref.at[slot],
            load_sem.at[slot],
        )

    load(0, 0).start()

    def place(k):
        return lax.rem(k, seqs) * groups + k // seqs

    def remote(src, dst, sems, which, k, index):
        return pltpu.make_async_remote_copy(
            src_ref=src,
            dst_ref=dst,
            send_sem=sems[0].at[which, k],
            recv_sem=sems[1].at[which, k],
            device_id=to(index),
            device_id_type=MESH,
        )

    def q_in(k):
        return remote(q_ref.at[place(k)], qin_ref.at[k], (in_send, in_recv), 0, k, partner)

    def g_in(k):
        return remote(g_ref.at[place(k)], gin_ref.at[k], (in_send, in_recv), 1, k, partner)

    def att_out(k):
        return remote(atts_ref.at[k], att_ref.at[place(k)], (out_send, out_recv), 0, k, partner)

    def dq_out(k):
        return remote(dqs_ref.at[k], dq_ref.at[place(k)], (out_send, out_recv), 1, k, partner)

    def given_of(s):
        return (count - s + seqs - 1) // seqs

    def start_in(s):
        def one(i, carry):
            q_in(i * seqs + s).start()
            g_in(i * seqs + s).start()
            return carry

        lax.fori_loop(0, upper * given_of(s), one, 0)

    start_in(0)

    sems = (sum_send, sum_recv, fill_sem, empty_sem)
    half_down, half_up = down_ref.shape[1] // 2, up_ref.shape[1] // 2
    teams = []
    for i in range(2):
        teams.append(
            [
                Exchange(
                    2 * i, orders[0], down_ref, sum_ref.at[0], down_acc_ref, down_recv_ref,
                    i * half_down, half_down, sems,
                ),
                Exchange(
                    2 * i + 1, orders[1], up_ref, sum_ref.at[1], up_acc_ref, up_recv_ref,
                    i * half_up, half_up, sems,
                ),
            ]
        )
    most_waits = [max(e.waits for e in team) for team in teams]
    acts = sorted(
        [(k + 1.5 * i, i, k) for i in range(2) for k in range(most_waits[i])]
    )
    acts = [(i, k) for _, i, k in acts]
    for team in teams:
        for e in team:
            e.begin()

    def act(number, carry):
        for n, (i, k) in enumerate(acts):
            def run(i=i, k=k):
                for e in teams[i]:
                    if k < e.waits:
                        e.take(k)

            pl.when(number == n)(run)
        return carry

    def cost_of(position):
        return position * rows // KEYS + 2

    total_cost = (tiles - upper * count) * cost_of(me) + (1 - upper) * count * cost_of(partner)

    def advance(acted, progress):
        due = jnp.minimum(progress * (len(acts) + 1) // total_cost, len(acts))
        lax.fori_loop(acted, due, act, 0)
        return jnp.maximum(acted, due)

    def core_out(s):
        return pltpu.make_async_remote_copy(
            src_ref=stage_ref.at[lax.rem(s, 2), :, 1 - core],
            dst_ref=half_ref.at[s],
            send_sem=core_send.at[s],
            recv_sem=core_recv.at[s],
            device_id=to(flip(me, 1)),
            device_id_type=MESH,
        )

    def slot_out(s, m):
        target = lax.rem(chip + m, chips)
        return pltpu.make_async_remote_copy(
            src_ref=half_ref.at[s, target],
            dst_ref=slot_ref.at[s, m],
            send_sem=slot_send.at[s, m],
            recv_sem=slot_recv.at[s, m],
            device_id=to(2 * target + core),
            device_id_type=MESH,
        )

    def slot_own(s):
        return pltpu.make_async_copy(half_ref.at[s, chip], slot_ref.at[s, 0], own_sem.at[s])

    def pass_on(s):
        core_out(s).wait()

        def add(m, carry):
            half_ref[s, m] = (
                half_ref[s, m].astype(F32) + stage_ref[lax.rem(s, 2), m, core].astype(F32)
            ).astype(BF)
            return carry

        lax.fori_loop(0, chips, add, 0)
        slot_own(s).start()
        for m in range(1, chips):
            slot_out(s, m).start()

    qs_ref[...] = jnp.zeros_like(qs_ref)
    gs_ref[...] = jnp.zeros_like(gs_ref)

    def at(b, n=1):
        return pl.ds(pl.multiple_of(b * KEYS, KEYS), n * KEYS)

    def blocks(count_blocks, body, state):
        state = lax.fori_loop(0, count_blocks // 4, lambda i, c: body(4 * i, 4, c), state)
        pairs = count_blocks // 2
        state = lax.fori_loop(
            count_blocks // 4 * 2, pairs, lambda i, c: body(2 * i, 2, c), state
        )
        return lax.fori_loop(2 * pairs, count_blocks, lambda i, c: body(i, 1, c), state)

    def spread(tile, out):
        for h in range(heads):
            tile[h * HEAD_DIM : (h + 1) * HEAD_DIM, :] = out[:, h * rows : (h + 1) * rows].astype(
                BF
            )

    def gather(tile, out):
        for h in range(heads):
            out[0:HEAD_DIM, h * rows : (h + 1) * rows] = tile[
                h * HEAD_DIM : (h + 1) * HEAD_DIM, :
            ]

    def tile(mine, t, k, position, acted, progress):
        start = position * rows
        edge = start // KEYS
        shift = lax.rem(start, KEYS)
        other = jnp.logical_not(mine)

        @pl.when(mine)
        def _():
            gather(q_ref.at[t], qs_ref)
            gather(g_ref.at[t], graw_ref)

        @pl.when(other)
        def _():
            q_in(k).wait_recv()
            g_in(k).wait_recv()
            gather(qin_ref.at[k], qs_ref)
            gather(gin_ref.at[k], graw_ref)

        s = dot(rows_ref[at(edge), :], qs_ref[...], 1, 0)
        column = lax.rem(lax.broadcasted_iota(jnp.int32, (1, lanes), 1), rows) + shift
        keep = lax.broadcasted_iota(jnp.int32, (KEYS, lanes), 0) <= column
        s = jnp.where(keep, s, -1e30)
        s_ref[at(edge), :] = s

        def top_of(s, n):
            return jnp.max(s.reshape(n * KEYS // 8, 8, lanes), axis=0)

        def scores(b, n, top):
            s = dot(rows_ref[at(b, n), :], qs_ref[...], 1, 0)
            s_ref[at(b, n), :] = s
            return jnp.maximum(top, top_of(s, n))

        top = jnp.max(blocks(edge, scores, top_of(s, 1)), axis=0, keepdims=True)

        def forward(b, n, state):
            total, out = state
            p = jnp.exp2(s_ref[at(b, n), :] - top)
            low = p.astype(BF)
            p_ref[at(b, n), :] = low
            return (
                total + jnp.sum(p.reshape(n * KEYS // 8, 8, lanes), axis=0),
                out + dot(flat_ref[HEAD_DIM : 2 * HEAD_DIM, at(b, n)], low, 1, 0),
            )

        total, out = blocks(
            edge + 1, forward, (jnp.zeros((8, lanes), F32), jnp.zeros((HEAD_DIM, lanes), F32))
        )
        inverse = 1.0 / jnp.sum(total, axis=0, keepdims=True)
        out = out * inverse
        pl.when(mine)(lambda: spread(att_ref.at[t], out))

        @pl.when(other)
        def _():
            spread(atts_ref.at[k], out)
            att_out(k).start()

        acted = advance(acted, progress + (edge + 2) // 2)
        g = graw_ref[...]
        scaled = (g.astype(F32) * inverse).astype(BF)
        gs_ref[HEAD_DIM : 2 * HEAD_DIM, :] = scaled
        delta = jnp.sum(scaled.astype(F32) * out, axis=0, keepdims=True)

        def backward(b, n, dq):
            p = p_ref[at(b, n), :]
            dp = dot(rows_ref[at(b, n), :], gs_ref[...], 1, 0)
            ds = (p.astype(F32) * (dp - delta)).astype(BF)
            dkv_ref[at(b, n), :] += dot(p, gs_ref[...], 1, 1) + dot(ds, qs_ref[...], 1, 1)
            return dq + dot(flat_ref[0:HEAD_DIM, at(b, n)], ds, 1, 0)

        dq = blocks(edge + 1, backward, jnp.zeros((HEAD_DIM, lanes), F32))
        dq = dq * (HEAD_DIM**-0.5)
        pl.when(mine)(lambda: spread(dq_ref.at[t], dq))

        @pl.when(other)
        def _():
            spread(dqs_ref.at[k], dq)
            dq_out(k).start()

        progress = progress + edge + 2
        return advance(acted, progress), progress

    per_block = KEYS // rows

    def sequence(s, state):
        slot = lax.rem(s, 2)
        load(s, slot).wait()
        pl.when(s + 1 < seqs)(lambda: load(s + 1, 1 - slot).start())
        dkv_ref[...] = jnp.zeros_like(dkv_ref)

        def turn(b, c):
            wide = jnp.concatenate(
                [kvt_ref[slot, b * per_block + i] for i in range(per_block)], axis=1
            )
            flat_ref[:, at(b)] = wide
            rows_ref[at(b), :] = wide.T
            return c

        lax.fori_loop(0, length // KEYS, turn, 0)
        given = given_of(s)
        own = groups - upper * given
        taken = (1 - upper) * given
        later = jnp.minimum(s, 1)

        def work(u, state):
            acted, progress = state
            v = u - taken * later
            mine = (v >= 0) & (v < own)
            t = s * groups + upper * given + jnp.clip(v, 0, own - 1)
            k = jnp.clip(u - own * (1 - later), 0, jnp.maximum(taken - 1, 0)) * seqs + s
            position = jnp.where(mine, me, partner)
            state = tile(mine, t, k, position, acted, progress)
            pl.when((u == 0) & (s > 0))(lambda: pass_on(s - 1))
            pl.when((u == 0) & (s + 1 < seqs))(lambda: start_in(s + 1))
            return state

        state = lax.fori_loop(0, own + taken, work, state)
        stage_ref[slot] = dkv_ref[...].reshape(chips, 2, rows, 2 * HEAD_DIM).astype(BF)
        core_out(s).start()
        return state

    acted, _ = lax.fori_loop(0, seqs, sequence, (jnp.int32(0), jnp.int32(0)))
    pass_on(seqs - 1)
    lax.fori_loop(acted, len(acts), act, 0)

    def end_given(k, c):
        q_in(k).wait_send()
        g_in(k).wait_send()
        att_out(k).wait_recv()
        dq_out(k).wait_recv()
        return c

    def end_taken(k, c):
        att_out(k).wait_send()
        dq_out(k).wait_send()
        return c

    lax.fori_loop(0, count * upper, end_given, 0)
    lax.fori_loop(0, count * (1 - upper), end_taken, 0)

    def end(s, c):
        slot_own(s).wait()
        for m in range(1, chips):
            slot_out(s, m).wait()
        return c

    lax.fori_loop(0, seqs, end, 0)


def attention(q, g, kv_all, down, up, seqs, dp):
    tiles, width, rows = q.shape
    ring = kv_all.shape[0]
    chips = ring // 2
    length = ring * rows
    lanes = width // HEAD_DIM * rows
    most = max(shipped(i, ring, tiles) for i in range(chips, ring))
    vmem = pl.BlockSpec(memory_space=pltpu.VMEM)
    anywhere = pl.BlockSpec(memory_space=pl.ANY)
    pair = 2 * HEAD_DIM
    dma = pltpu.SemaphoreType.DMA
    orders = bit_orders(dp, ring)
    stages = len(orders[0])
    return pl.pallas_call(
        functools.partial(attention_kernel, seqs, tiles // seqs, orders),
        out_shape=[
            jax.ShapeDtypeStruct(q.shape, BF),
            jax.ShapeDtypeStruct(q.shape, BF),
            jax.ShapeDtypeStruct((seqs, chips, rows, pair), BF),
            jax.ShapeDtypeStruct(
                (2, down.shape[0] >> halvings_of(down.shape[0], stages), down.shape[1]), BF
            ),
        ],
        in_specs=[vmem, vmem, anywhere, anywhere, anywhere],
        out_specs=[vmem, vmem, anywhere, anywhere],
        scratch_shapes=[
            pltpu.VMEM((2, ring, pair, rows), BF),
            pltpu.VMEM((pair, length), BF),
            pltpu.VMEM((length, pair), BF),
            pltpu.VMEM((length, pair), F32),
            pltpu.VMEM((length, lanes), F32),
            pltpu.VMEM((length, lanes), BF),
            pltpu.VMEM((pair, lanes), BF),
            pltpu.VMEM((pair, lanes), BF),
            pltpu.VMEM((most, width, rows), BF),
            pltpu.VMEM((most, width, rows), BF),
            pltpu.VMEM((most, width, rows), BF),
            pltpu.VMEM((most, width, rows), BF),
            pltpu.VMEM((2, chips, 2, rows, pair), BF),
            pltpu.VMEM((seqs, chips, rows, pair), BF),
            dma((2,)),
            dma((seqs,)),
            dma((2, most)),
            dma((2, most)),
            dma((2, most)),
            dma((2, most)),
            dma((seqs,)),
            dma((seqs,)),
            dma((seqs, chips)),
            dma((seqs, chips)),
            pltpu.VMEM((down.shape[0] // 2, down.shape[1]), BF),
            pltpu.VMEM((up.shape[0] // 2, up.shape[1]), BF),
            pltpu.VMEM((exchange_rows(down.shape[0], stages), down.shape[1]), BF),
            pltpu.VMEM((exchange_rows(up.shape[0], stages), up.shape[1]), BF),
            pltpu.VMEM((HEAD_DIM, lanes), BF),
            dma((4, stages)),
            dma((4, stages)),
            dma((4,)),
            dma((4,)),
        ],
        compiler_params=pltpu.CompilerParams(
            collective_id=2, has_side_effects=True, vmem_limit_bytes=60 * 2**20
        ),
        cost_estimate=pl.CostEstimate(
            flops=12 * tiles * rows * width * length * 4,
            bytes_accessed=8 * q.size,
            transcendentals=tiles * lanes * length // 2,
        ),
        name="attention",
    )(q, g, kv_all, down, up)


def bit_orders(dp, ring):
    seq_bits = [("seq", 1 << b) for b in range(ring.bit_length() - 1)]
    dp_bits = [("dp", 1 << b) for b in range(dp.bit_length() - 1)]
    far = seq_bits[2:]
    return (seq_bits[:2] + dp_bits + far, seq_bits[:1] + dp_bits + seq_bits[1:2] + far)

def side_of(bit):
    axis, weight = bit
    return lax.rem(lax.axis_index(axis) // weight, 2)

def partner_of(bit):
    axis, weight = bit
    me = lax.axis_index(axis)
    return {axis: me + weight - 2 * weight * side_of(bit)}

def add_rows(dst, a, b, dst_at, a_at, rows, step):
    def body(i, carry):
        r = pl.multiple_of(i * step, step)
        dst[pl.ds(dst_at + r, step), :] = a[pl.ds(a_at + r, step), :] + b[pl.ds(r, step), :]
        return carry
    lax.fori_loop(0, rows // step, body, 0)

def sum_kernel(orders, x_ref, out_ref, *scratch):
    parts = len(orders)
    stages = len(orders[0])
    rows, cols = x_ref.shape
    wide = cols // parts
    acc, recv, sems = scratch[:parts], scratch[parts:2*parts], scratch[2*parts:]
    send_sem, recv_sem = sems
    barrier = pltpu.get_barrier_semaphore()
    for bit in orders[0]:
        pl.semaphore_signal(barrier, inc=1, device_id=partner_of(bit), device_id_type=MESH)
    pl.semaphore_wait(barrier, stages)
    def copy(p, s, src, dst, bit):
        return pltpu.make_async_remote_copy(src_ref=src, dst_ref=dst, send_sem=send_sem.at[p, s], recv_sem=recv_sem.at[p, s],
            device_id=partner_of(bit), device_id_type=MESH)
    columns = [pl.ds(p * wide, wide) for p in range(parts)]
    start = [0] * parts
    whole = [0] * parts
    live = {}
    base = [0]
    for s in range(stages): base.append(base[-1] + rows // 2 ** min(s + 1, stages - 1))
    def launch(p, s):
        bit = orders[p][s]
        if s < stages - 1:
            half = rows // 2 ** (s + 1)
            other = pl.multiple_of(start[p] + (1 - side_of(bit)) * half, half)
            src = x_ref.at[pl.ds(other, half), columns[p]] if s == 0 else acc[p].at[pl.ds(other, half), :]
        else:
            half = rows // 2 ** s
            src = acc[p].at[pl.ds(pl.multiple_of(start[p], half), half), :]
        live[p] = copy(p, s, src, recv[p].at[pl.ds(base[s], half), :], bit)
        live[p].start()
    for p in range(parts): launch(p, 0)
    for s in range(stages):
        for p in range(parts):
            bit = orders[p][s]
            live[p].wait()
            half = rows // 2 ** min(s + 1, stages - 1)
            step = 16 if half % 64 else 64
            got = recv[p].at[pl.ds(base[s], half), :]
            if s == 0:
                mine = side_of(bit) * half
                whole[p] = mine
                add_rows(acc[p], x_ref.at[:, columns[p]], got, 0, pl.multiple_of(mine, half), half, step)
                start[p] = 0
            elif s < stages - 1:
                mine = pl.multiple_of(start[p] + side_of(bit) * half, half)
                add_rows(acc[p], acc[p], got, mine, mine, half, step)
                whole[p] = whole[p] + side_of(bit) * half
                start[p] = start[p] + side_of(bit) * half
            else:
                at = pl.multiple_of(start[p], half)
                add_rows(out_ref.at[:, columns[p]], acc[p], got, pl.multiple_of(whole[p], half), at, half, step)
            if s < stages - 1: launch(p, s + 1)
    def spread(p, s):
        bit = orders[p][s]
        half = rows // 2 ** (s + 1)
        src = out_ref.at[pl.ds(pl.multiple_of(whole[p], half), half), columns[p]]
        live[p] = copy(p, 2 * stages - 2 - s, src, src, bit)
        live[p].start()
    for p in range(parts): spread(p, stages - 2)
    for s in range(stages - 2, -1, -1):
        for p in range(parts):
            live[p].wait()
            whole[p] = whole[p] - side_of(orders[p][s]) * (rows // 2 ** (s + 1))
            if s: spread(p, s - 1)

def total_of(x, dp, ring, collective_id):
    orders = bit_orders(dp, ring)
    rows, cols = x.shape
    parts, stages = len(orders), len(orders[0])
    wide = cols // parts
    got = sum(rows // 2 ** min(s + 1, stages - 1) for s in range(stages))
    whole = pl.BlockSpec(memory_space=pltpu.VMEM)
    return pl.pallas_call(functools.partial(sum_kernel, orders),
        out_shape=jax.ShapeDtypeStruct(x.shape, BF), in_specs=[whole], out_specs=whole,
        scratch_shapes=[pltpu.VMEM((rows // 2, wide), BF)] * parts + [pltpu.VMEM((got, wide), BF)] * parts
        + [pltpu.SemaphoreType.DMA((parts, 2 * stages - 1))] * 2,
        compiler_params=pltpu.CompilerParams(collective_id=collective_id, has_side_effects=True, vmem_limit_bytes=56*2**20),
        name="total")(x)


def normal(h):
    center = h - jnp.mean(h, axis=-1, keepdims=True)
    spread = jnp.mean(center * center, axis=-1, keepdims=True)
    inverse = lax.rsqrt(spread + 1e-05)
    return center * inverse, inverse


def norm_gradient(q, gain, n, inverse):
    scaled = q * gain
    inner = jnp.mean(scaled * n, axis=-1, keepdims=True)
    return inverse * (scaled - jnp.mean(scaled, axis=-1, keepdims=True) - n * inner)


def turned_back(rows, cosine, sine):
    half = cosine.shape[0]
    first, second = rows[:half], rows[half : 2 * half]
    return jnp.concatenate(
        [first * cosine + second * sine, second * cosine - first * sine, rows[2 * half :]], axis=0
    )


def finish_kernel(
    att_ref,
    dq_ref,
    slot_ref,
    cos_ref,
    sin_ref,
    h_ref,
    c_ref,
    ff_ref,
    gm_ref,
    norms_ref,
    weight_ref,
    out_weight_ref,
    up_bias_ref,
    layer_ref,
    input_ref,
    rest_ref,
    raw_ref,
    acc_ref,
    lines_ref,
):
    step = pl.program_id(0)
    d = h_ref.shape[1]
    rows = h_ref.shape[0]
    wide = weight_ref.shape[1]

    @pl.when(step == 0)
    def _():
        acc_ref[...] = jnp.zeros_like(acc_ref)
        lines_ref[...] = jnp.zeros_like(lines_ref)
        for i in range(up_bias_ref.shape[1] // d):
            lines_ref[8 + i : 9 + i, :] = up_bias_ref[:, i * d : (i + 1) * d]

    hidden = h_ref[...].astype(F32)
    low_c = c_ref[...]
    cot = low_c.astype(F32)
    n, inverse = normal(hidden)
    gain1, bias1 = norms_ref[0:1, :], norms_ref[1:2, :]
    gain2, bias_out = norms_ref[2:3, :], norms_ref[3:4, :]
    normed = (n * gain1 + bias1).astype(BF)
    att = att_ref[0]
    layer_ref[...] = hidden + dot(att, out_weight_ref[...], 0, 0) + ff_ref[...] + bias_out
    acc_ref[wide : wide + d, :] += dot(att, low_c, 1, 0)
    cosine, sine = cos_ref[0], sin_ref[0]
    for h in range(d // HEAD_DIM):
        at = slice(h * HEAD_DIM, (h + 1) * HEAD_DIM)
        raw_ref[at, :] = turned_back(dq_ref[0, at, :].astype(F32), cosine, sine).astype(BF)
    kv = slot_ref[0, 0].astype(F32)
    for m in range(1, slot_ref.shape[1]):
        kv = kv + slot_ref[0, m].astype(F32)
    lane = lax.broadcasted_iota(jnp.int32, (1, 2 * HEAD_DIM), 1)
    kv = (kv * jnp.where(lane < HEAD_DIM, 1.0 / LOG2E, 1.0)).astype(BF).astype(F32).T
    raw_ref[d : d + HEAD_DIM, :] = turned_back(kv[:HEAD_DIM], cosine, sine).astype(BF)
    raw_ref[d + HEAD_DIM :, :] = kv[HEAD_DIM:].astype(BF)
    raw = raw_ref[...]
    acc_ref[0:wide, :] += dot(raw, normed, 1, 0)
    sums = dot(jnp.ones((8, rows), BF), raw, 1, 1)
    lines_ref[4:5, :] += sums[0:1, :d]
    lines_ref[5:6, 0 : wide - d] += sums[0:1, d:]
    ga = dot(raw, weight_ref[...], 0, 1)
    gm = gm_ref[...]
    lines_ref[0:1, :] += jnp.sum(ga * n, axis=0, keepdims=True)
    lines_ref[1:2, :] += jnp.sum(ga, axis=0, keepdims=True)
    lines_ref[2:3, :] += jnp.sum(gm * n, axis=0, keepdims=True)
    lines_ref[3:4, :] += jnp.sum(gm, axis=0, keepdims=True)
    lines_ref[6:7, :] += jnp.sum(cot, axis=0, keepdims=True)
    input_ref[...] = (
        cot + norm_gradient(ga, gain1, n, inverse) + norm_gradient(gm, gain2, n, inverse)
    )

    @pl.when(step == pl.num_programs(0) - 1)
    def _():
        rest_ref[0:d, :] = acc_ref[0:d, :].T.astype(BF)
        rest_ref[d : 2 * d, :] = acc_ref[wide : wide + d, :].astype(BF)
        rest_ref[2 * d : d + wide, :] = acc_ref[d:wide, :].astype(BF)
        rest_ref[d + wide : d + wide + 16, :] = lines_ref[...].astype(BF)
        rest_ref[d + wide + 16 :, :] = jnp.zeros((rest_ref.shape[0] - d - wide - 16, d), BF)


def finish(att, dq, slots, cosine, sine, hidden, cot, ff, gm, norms, weight, out_weight, up_bias, padded):
    seqs, d, rows = att.shape
    wide = weight.shape[1]
    by_seq = pl.BlockSpec((1, d, rows), lambda i: (i, 0, 0))
    angle = pl.BlockSpec((1,) + cosine.shape[1:], lambda i: (i, 0, 0))
    by_row = pl.BlockSpec((rows, d), lambda i: (i, 0))

    def all_of(a):
        return pl.BlockSpec(a.shape, lambda i: (0,) * a.ndim)

    return pl.pallas_call(
        finish_kernel,
        grid=(seqs,),
        out_shape=[
            jax.ShapeDtypeStruct(hidden.shape, F32),
            jax.ShapeDtypeStruct(hidden.shape, F32),
            jax.ShapeDtypeStruct((padded, d), BF),
        ],
        in_specs=[
            by_seq,
            by_seq,
            pl.BlockSpec((1,) + slots.shape[1:], lambda i: (i, 0, 0, 0)),
            angle,
            angle,
            by_row,
            by_row,
            by_row,
            by_row,
            all_of(norms),
            all_of(weight),
            all_of(out_weight),
            all_of(up_bias),
        ],
        out_specs=[by_row, by_row, pl.BlockSpec((padded, d), lambda i: (0, 0))],
        scratch_shapes=[
            pltpu.VMEM((wide, rows), BF),
            pltpu.VMEM((wide + d, d), F32),
            pltpu.VMEM((16, d), F32),
        ],
        compiler_params=pltpu.CompilerParams(vmem_limit_bytes=48 * 2**20),
        cost_estimate=pl.CostEstimate(
            flops=12 * seqs * rows * d * d, bytes_accessed=26 * seqs * rows * d, transcendentals=0
        ),
        name="finish",
    )(att, dq, slots, cosine, sine, hidden, cot, ff, gm, norms, weight, out_weight, up_bias)


def local(
    hidden_in,
    positions,
    ln1_gain,
    ln1_bias,
    ln2_gain,
    ln2_bias,
    query_projection,
    query_bias,
    shared_key_weight,
    shared_key_bias,
    shared_value_weight,
    shared_value_bias,
    output_weight,
    output_bias,
    up_weight,
    up_bias,
    down_weight,
    down_bias,
    cotangent,
):
    seq_count, local_len = hidden_in.shape[0], hidden_in.shape[1]
    ring = lax.axis_size("seq")
    groups = ring // seq_count
    per_group = HEADS // groups
    width = per_group * HEAD_DIM
    hidden = hidden_in.astype(F32)
    cosine, sine = angles_of(positions)
    normed_a = layer_norm(hidden, ln1_gain, ln1_bias).astype(BF)
    normed_m = layer_norm(hidden, ln2_gain, ln2_bias).astype(BF)

    tokens = seq_count * local_len
    kv_weight = jnp.concatenate([shared_key_weight, shared_value_weight], axis=1)
    kv_bias = jnp.concatenate([shared_key_bias, shared_value_bias])
    kv_pre = jnp.einsum("stc,cw->swt", normed_a, kv_weight, preferred_element_type=F32)
    kv_pre = kv_pre + kv_bias[:, None]
    kv_low = jnp.concatenate(
        [rotary_rows(kv_pre[:, :HEAD_DIM], cosine, sine), kv_pre[:, HEAD_DIM:]], axis=1
    ).astype(BF)
    kv_all = lax.all_gather(kv_low.reshape(-1, local_len), "seq")
    query_pre = jnp.einsum("stc,cw->swt", normed_a, query_projection, preferred_element_type=F32)
    query_pre = (query_pre + query_bias[:, None]).reshape(seq_count, HEADS, HEAD_DIM, local_len)
    query_low = (rotary_rows(query_pre, cosine[:, None], sine[:, None]) * (LOG2E / 8.0)).astype(BF)
    query_tiles = query_low.reshape(-1, width, local_len)
    grad_attended = jnp.einsum(
        "stc,wc->swt", cotangent, output_weight, preferred_element_type=F32
    ).astype(BF)
    grad_tiles = grad_attended.reshape(-1, width, local_len)

    feedforward, grad_normed_m, grad_w_up, grad_w_down, grad_b_up = feed_forward(
        normed_m.reshape(tokens, D),
        cotangent.reshape(tokens, D),
        up_weight,
        up_bias[None],
        down_weight,
    )
    query_tiles, grad_tiles, kv_all, grad_w_up, grad_w_down = lax.optimization_barrier(
        (query_tiles, grad_tiles, kv_all, grad_w_up, grad_w_down)
    )
    dp = lax.axis_size("dp")
    orders = bit_orders(dp, ring)
    out, dq, dkv, parts = attention(
        query_tiles, grad_tiles, kv_all, grad_w_down, grad_w_up, seq_count, dp
    )
    grad_w_down, grad_w_up = unpack(
        parts, down_weight.shape, up_weight.shape, orders, dp, ring
    )
    qkv = D + 2 * HEAD_DIM
    ff = up_weight.shape[1]
    unit = 16 * dp * ring // 2
    padded = -(-(D + qkv + 16) // unit) * unit
    norms = jnp.concatenate(
        [ln1_gain[None], ln1_bias[None], ln2_gain[None], (output_bias + down_bias)[None]]
        + [jnp.zeros((4, D), F32)],
        axis=0,
    )
    layer_out, input_grad, rest = finish(
        out.reshape(seq_count, D, local_len),
        dq.reshape(seq_count, D, local_len),
        dkv,
        cosine,
        sine,
        hidden_in.reshape(tokens, D),
        cotangent.reshape(tokens, D),
        feedforward,
        grad_normed_m,
        norms,
        jnp.concatenate([query_projection, kv_weight], axis=1),
        output_weight,
        grad_b_up,
        padded,
    )
    rest = total_of(rest, dp, ring, 3)
    kv_rows = rest[2 * D : D + qkv].astype(F32)
    lines = rest[D + qkv : D + qkv + 16].astype(F32)
    return (
        layer_out.reshape(hidden.shape),
        input_grad.reshape(hidden.shape),
        lines[0],
        lines[1],
        lines[2],
        lines[3],
        rest[:D].astype(F32),
        lines[4],
        kv_rows[:HEAD_DIM].T,
        lines[5, :HEAD_DIM],
        kv_rows[HEAD_DIM:].T,
        lines[5, HEAD_DIM : 2 * HEAD_DIM],
        rest[D : 2 * D].astype(F32),
        lines[6],
        grad_w_up,
        lines[8 : 8 + ff // D].reshape(ff),
        grad_w_down,
        lines[6],
    )


def solution(mesh):
    rows = P("dp", "seq", None)
    placed = (rows, P("dp", "seq")) + (P(),) * 16 + (rows,)
    return jax.shard_map(
        local,
        mesh=mesh,
        in_specs=placed,
        out_specs=(rows, rows) + (P(),) * 16,
        check_vma=False,
    )
```

profile of v0, /device:TPU:0, one launch (start us, length us, event | category | flops | bytes accessed | tf_op | source)
XLA Modules:
  0.0 350.3 jit_solution(15476679465794545142)
XLA Ops:
  7.2 0.0 copy-start.5
  7.2 0.0 copy-start.19
  7.2 0.0 copy-start.17
  7.2 0.0 copy-start.9
  7.3 0.0 copy-start.7
  7.3 0.0 all-gather.4.cloned.1.call-start
  7.3 0.8 convert_element_type.57
  8.1 1.7 convert_reduce_fusion
  9.8 2.0 fusion.8
  11.8 0.1 pad_maximum_fusion.2
  12.0 0.0 copy-start.22
  12.0 0.9 fusion.10
  12.9 0.2 subtract_convert_fusion
  13.1 0.7 pad_maximum_fusion.1
  13.9 0.0 all-gather.4.cloned.1.call-update
  13.9 0.0 all-gather.6.cloned.1.call-start
  14.0 3.3 add_bitcast_fusion
  17.3 3.5 %copy.45 = f32[4,768,256]{2,1,0:T(8,128)} copy(f32[4,768,256]{1,2,0:T(8,128)} %add_bitcast_fusion) | data formatting | bytes 6291456 | tf_op jit(solution)/shard_map/add | solution.py:1052
  20.8 1.8 slice.94
  22.7 1.2 multiply_subtract_fusion
  23.9 0.0 copy-start
  23.9 1.6 fusion.9
  25.5 1.8 fusion.7
  27.3 2.6 convolution_convert_fusion
  29.9 41.0 %feed_forward.1 = (f32[1024,768]{1,0:T(8,128)}, f32[1024,768]{1,0:T(8,128)}, bf16[3072,768]{1,0:T(8,128)(2,1)}, bf16[3072,768]{1,0:T(8,128)(2,1)}, f32[1,3072]{1,0:T(1,128)}) custom-call(bf16[1024,768]{1,0:T(8,128)(2,1)} %bitcast.43, bf16[1024,768]{1,0:T(8,128)(2,1)} %bitcast.46, bf16[768,3072]{1,0:T(8,128)(2,1)} %up_ref.1, bf16[3072,768]{1,0:T(8,128)(2,1)} %down_ref.1, ...), custom_call_target="tpu_custom_call" | custom-call | flops 28991029248 | bytes 37748736 | tf_op jit(solution)/shard_map/feed_forward/pallas_call | solution.py:116
  70.9 0.0 all-gather.4.cloned.1.call-done.all_ref
  70.9 0.0 copy-start.18
  70.9 0.0 copy-start.20
  70.9 0.0 copy-start.15
  71.0 0.0 copy-start.16
  71.0 154.7 %attention.1 = (bf16[16,192,256]{2,1,0:T(8,128)(2,1)}, bf16[16,192,256]{2,1,0:T(8,128)(2,1)}, bf16[4,8,256,128]{3,2,1,0:T(8,128)(2,1)}, bf16[2,96,768]{2,1,0:T(8,128)(2,1)}) custom-call(bf16[16,192,256]{2,1,0:T(8,128)(2,1)} %bitcast.44, bf16[16,192,256]{2,1,0:T(8,128)(2,1)} %bitcast.51, bf16[16,512,256]{2,1,0:T(8,128)(2,1)} %all-gather.4.cloned.1.call-done.all_ref, ...), custom_call_target="tpu_custom_call" | custom-call | flops 154618822656 | bytes 6291456 | tf_op jit(solution)/shard_map/attention/pallas_call | solution.py:702
  225.7 0.0 all-gather.6.cloned.1.call-update
  225.8 0.2 copy.46
  226.0 0.2 copy.47
  226.3 1.7 pad_maximum_fusion.weight_ref
  228.0 1.4 copy-done.3
  229.4 14.6 %finish.1 = (f32[1024,768]{1,0:T(8,128)}, f32[1024,768]{1,0:T(8,128)}, bf16[1792,768]{1,0:T(8,128)(2,1)}) custom-call(bf16[4,768,256]{2,1,0:T(8,128)(2,1)S(1)} %bitcast.37, bf16[4,768,256]{2,1,0:T(8,128)(2,1)S(1)} %bitcast.38, bf16[4,8,256,128]{3,2,1,0:T(8,128)(2,1)} %get-tuple-element.46.slot_ref, f32[4,8,256]{2,1,0:T(8,128)S(1)} %get-tuple-element.73.cos_ref, ...), custom_call_target="tpu_custom_call" | custom-call | flops 7247757312 | bytes 20447232 | tf_op jit(solution)/shard_map/finish/pallas_call | solution.py:974
  244.1 79.9 %total.1 = bf16[1792,768]{1,0:T(8,128)(2,1)} custom-call(bf16[1792,768]{1,0:T(8,128)(2,1)} %get-tuple-element.52.x_ref), custom_call_target="tpu_custom_call" | custom-call | tf_op jit(solution)/shard_map/total/pallas_call | solution.py:856
  324.0 0.7 slice_convert_fusion.4
  324.7 0.6 reshape.120
  325.3 0.6 slice_reduce_fusion
  326.0 0.6 slice_bitcast_fusion.2
  326.6 1.0 slice_convert_fusion.3
  327.5 0.8 slice_bitcast_fusion
  328.3 4.3 %slice_convert_fusion = (f32[768,768]{1,0:T(8,128)}, f32[768,768]{1,0:T(8,128)}) fusion(bf16[1792,768]{1,0:T(8,128)(2,1)} %total.1), kind=kLoop, calls=%fused_computation.20 | loop fusion | flops 1179648 | bytes 7077888 | tf_op jit(solution)/shard_map/convert_element_type | solution.py:1119
  332.6 0.0 all-gather.6.cloned.1.call-done
  332.7 10.2 %unpack.1 = (f32[3072,768]{1,0:T(8,128)}, f32[768,3072]{1,0:T(8,128)}) custom-call(bf16[32,2,96,768]{3,2,1,0:T(8,128)(2,1)} %bitcast.42), custom_call_target="tpu_custom_call" | custom-call | flops 9437184 | bytes 28311552 | tf_op jit(solution)/shard_map/unpack/pallas_call | solution.py:278
  342.9 0.6 copy.49
  (50 shorter events, 0.2 us)
Async XLA Ops:
  7.2 4.7 %copy-start.5 = (bf16[4,256,768]{2,1,0:T(8,128)(2,1)S(1)}, bf16[4,256,768]{2,1,0:T(8,128)(2,1)}, u32[]{:S(2)}) copy-start(bf16[4,256,768]{2,1,0:T(8,128)(2,1)} %param.19) | copy-start | bytes 4718596
  7.2 4.6 %copy-start.23 = (f32[64]{0:T(128)S(1)}, f32[64]{0:T(128)}, u32[]{:S(2)}) copy-start(f32[64]{0:T(128)} %param.30) | copy-start | bytes 772
  7.2 4.6 %copy-start.24 = (f32[64]{0:T(128)S(1)}, f32[64]{0:T(128)}, u32[]{:S(2)}) copy-start(f32[64]{0:T(128)} %param.28) | copy-start | bytes 772
  7.2 4.7 %copy-start.19 = (f32[768]{0:T(1024)S(1)}, f32[768]{0:T(1024)}, u32[]{:S(2)}) copy-start(f32[768]{0:T(1024)} %param.22) | copy-start | bytes 9220
  7.2 4.7 %copy-start.17 = (f32[768]{0:T(1024)S(1)}, f32[768]{0:T(1024)}, u32[]{:S(2)}) copy-start(f32[768]{0:T(1024)} %param.21) | copy-start | bytes 9220
  7.2 4.7 %copy-start.9 = (bf16[768,64]{0,1:T(8,128)(2,1)S(1)}, bf16[768,64]{0,1:T(8,128)(2,1)}, u32[]{:S(2)}) copy-start(bf16[768,64]{0,1:T(8,128)(2,1)} %param.29) | copy-start | bytes 294916
  7.3 4.7 %copy-start.7 = (bf16[768,64]{0,1:T(8,128)(2,1)S(1)}, bf16[768,64]{0,1:T(8,128)(2,1)}, u32[]{:S(2)}) copy-start(bf16[768,64]{0,1:T(8,128)(2,1)} %param.27) | copy-start | bytes 294916
  7.3 63.6 %all-gather.4.cloned.1.call-start = ((), (), s32[]{:S(2)}) async-start(), calls=%async_computation | async-start | bytes 4456448 | tf_op jit(solution)/shard_map/all_gather | solution.py:1050
  11.9 2.0 copy-start.6
  12.0 2.0 copy-start.22
  13.9 318.8 %all-gather.6.cloned.1.call-start = ((), (), s32[]{:S(2)}) async-start(), calls=%async_computation.1 | async-start | bytes 9732096 | tf_op jit(solution)/shard_map/all_gather | solution.py:272
  22.7 2.9 copy-start.11
  22.7 2.9 copy-start.14
  23.9 3.4 copy-start
  23.9 3.4 copy-start.21
  70.9 154.9 %copy-start.12 = (f32[768]{0:T(1024)S(1)}, f32[768]{0:T(1024)}, u32[]{:S(2)}) copy-start(f32[768]{0:T(1024)} %param.23) | copy-start | bytes 9220
  70.9 154.9 %copy-start.18 = (f32[768]{0:T(1024)S(1)}, f32[768]{0:T(1024)}, u32[]{:S(2)}) copy-start(f32[768]{0:T(1024)} %param.21) | copy-start | bytes 9220
  70.9 154.9 %copy-start.20 = (f32[768]{0:T(1024)S(1)}, f32[768]{0:T(1024)}, u32[]{:S(2)}) copy-start(f32[768]{0:T(1024)} %param.22) | copy-start | bytes 9220
  70.9 154.9 %copy-start.8 = (bf16[768,64]{0,1:T(8,128)(2,1)S(1)}, bf16[768,64]{0,1:T(8,128)(2,1)}, u32[]{:S(2)}) copy-start(bf16[768,64]{0,1:T(8,128)(2,1)} %param.27) | copy-start | bytes 294916
  70.9 155.1 %copy-start.10 = (bf16[768,64]{0,1:T(8,128)(2,1)S(1)}, bf16[768,64]{0,1:T(8,128)(2,1)}, u32[]{:S(2)}) copy-start(bf16[768,64]{0,1:T(8,128)(2,1)} %param.29) | copy-start | bytes 294916
  70.9 155.3 %copy-start.15 = (f32[768]{0:T(1024)S(1)}, f32[768]{0:T(1024)}, u32[]{:S(2)}) copy-start(f32[768]{0:T(1024)} %param.32) | copy-start | bytes 9220
  71.0 155.3 %copy-start.16 = (f32[768]{0:T(1024)S(1)}, f32[768]{0:T(1024)}, u32[]{:S(2)}) copy-start(f32[768]{0:T(1024)} %param.36) | copy-start | bytes 9220
  225.7 2.3 copy-start.1
  225.7 2.3 copy-start.2
  225.7 2.3 copy-start.4
  228.0 1.4 copy-start.3
  326.0 16.9 %copy-start.13 = (f32[768]{0:T(1024)}, f32[768]{0:T(1024)S(1)}, u32[]{:S(2)}) copy-start(f32[768]{0:T(1024)S(1)} %get-tuple-element.109) | copy-start | bytes 9220
Sparse Core Ops, SparseCore 0:
  14.0 53.4 all-gather.3
  225.9 106.7 all-gather.5
where the time goes:
time: 351 us; the launch traced here: 350 us
  Pallas kernels  300 us (85%)
  other arithmetic  17.8 us (5%)
  between operations  14.5 us (4%)
  local copies, waits for them, and re-layouts  10.5 us (3%)
  matrix products  6.8 us (2%)
    pallas_call x1, Pallas kernels, attention(): pl.pallas_call(functools.partial(attention_kernel, seqs, tiles // seqs, o...  155 us
    pallas_call x1, Pallas kernels, total_of(): pl.pallas_call(functools.partial(sum_kernel, orders), out_shape=jax.Shape...  79.9 us
    pallas_call x1, Pallas kernels, feed_forward(): pl.pallas_call(feed_kernel, grid=(steps,), out_shape=[jax.ShapeDtypeStruc...  41 us
    pallas_call x1, Pallas kernels, finish(): pl.pallas_call(finish_kernel, grid=(seqs,), out_shape=[jax.ShapeDtypeStru...  14.6 us
    pallas_call x1, Pallas kernels, unpack(): pl.pallas_call(functools.partial(unpack_kernel, froms), out_shape=[jax.Sh...  10.2 us
  transfers between devices with their start and end apart: 2, of which 0 were waited for; matrix products, arithmetic and copies ran while one was open for 8% of the time, Pallas kernels for 39%

commit v1 on v0

--- a/solution.py
+++ b/solution.py
@@ -446,9 +446,13 @@
             ]
         )
     most_waits = [max(e.waits for e in team) for team in teams]
-    acts = sorted(
-        [(k + 1.5 * i, i, k) for i in range(2) for k in range(most_waits[i])]
-    )
+    planned = ((10, 40, 58, 72, 86), (18, 58, 76, 90, 101))
+    acts = []
+    for i in range(2):
+        for k in range(most_waits[i]):
+            acts.append((planned[i][min(k, 4)] + max(0, k - 4), i, k))
+    acts.sort()
+    dues = [due for due, _, _ in acts]
     acts = [(i, k) for _, i, k in acts]
     for team in teams:
         for e in team:
@@ -470,7 +474,7 @@
     total_cost = (tiles - upper * count) * cost_of(me) + (1 - upper) * count * cost_of(partner)
 
     def advance(acted, progress):
-        due = jnp.minimum(progress * (len(acts) + 1) // total_cost, len(acts))
+        due = sum(jnp.where(progress * 100 >= at * total_cost, 1, 0) for at in dues)
         lax.fori_loop(acted, due, act, 0)
         return jnp.maximum(acted, due)
 
@@ -773,92 +777,128 @@
     me = lax.axis_index(axis)
     return {axis: me + weight - 2 * weight * side_of(bit)}
 
-def add_rows(dst, a, b, dst_at, a_at, rows, step):
+def add_rows(dst, a, b, dst_at, a_at, rows):
+    step = next(n for n in (128, 96, 64, 48, 32, 16) if rows % n == 0)
+
     def body(i, carry):
         r = pl.multiple_of(i * step, step)
         dst[pl.ds(dst_at + r, step), :] = a[pl.ds(a_at + r, step), :] + b[pl.ds(r, step), :]
         return carry
+
     lax.fori_loop(0, rows // step, body, 0)
 
-def sum_kernel(orders, x_ref, out_ref, *scratch):
-    parts = len(orders)
+
+def sum_kernel(orders, spans, x_ref, out_ref, *scratch):
+    parts = [(order, i, span) for span in spans for i, order in enumerate(orders)]
+    count = len(parts)
     stages = len(orders[0])
-    rows, cols = x_ref.shape
-    wide = cols // parts
-    acc, recv, sems = scratch[:parts], scratch[parts:2*parts], scratch[2*parts:]
-    send_sem, recv_sem = sems
+    wide = x_ref.shape[1] // len(orders)
+    acc, recv = scratch[:count], scratch[count : 2 * count]
+    send_sem, recv_sem = scratch[2 * count :]
     barrier = pltpu.get_barrier_semaphore()
     for bit in orders[0]:
         pl.semaphore_signal(barrier, inc=1, device_id=partner_of(bit), device_id_type=MESH)
     pl.semaphore_wait(barrier, stages)
+
     def copy(p, s, src, dst, bit):
-        return pltpu.make_async_remote_copy(src_ref=src, dst_ref=dst, send_sem=send_sem.at[p, s], recv_sem=recv_sem.at[p, s],
-            device_id=partner_of(bit), device_id_type=MESH)
-    columns = [pl.ds(p * wide, wide) for p in range(parts)]
-    start = [0] * parts
-    whole = [0] * parts
+        return pltpu.make_async_remote_copy(
+            src_ref=src,
+            dst_ref=dst,
+            send_sem=send_sem.at[p, s],
+            recv_sem=recv_sem.at[p, s],
+            device_id=partner_of(bit),
+            device_id_type=MESH,
+        )
+
+    start = [0] * count
+    place = [0] * count
     live = {}
-    base = [0]
-    for s in range(stages): base.append(base[-1] + rows // 2 ** min(s + 1, stages - 1))
+
+    def size(p, s):
+        return parts[p][2][1] // 2 ** min(s + 1, stages - 1)
+
+    def base(p, s):
+        return sum(size(p, t) for t in range(s))
+
+    def view(ref, p):
+        _, i, (first, rows) = parts[p]
+        return ref.at[pl.ds(first, rows), pl.ds(i * wide, wide)]
+
     def launch(p, s):
-        bit = orders[p][s]
+        bit = parts[p][0][s]
+        half = size(p, s)
         if s < stages - 1:
-            half = rows // 2 ** (s + 1)
             other = pl.multiple_of(start[p] + (1 - side_of(bit)) * half, half)
-            src = x_ref.at[pl.ds(other, half), columns[p]] if s == 0 else acc[p].at[pl.ds(other, half), :]
+            src = (view(x_ref, p) if s == 0 else acc[p]).at[pl.ds(other, half), :]
         else:
-            half = rows // 2 ** s
             src = acc[p].at[pl.ds(pl.multiple_of(start[p], half), half), :]
-        live[p] = copy(p, s, src, recv[p].at[pl.ds(base[s], half), :], bit)
+        live[p] = copy(p, s, src, recv[p].at[pl.ds(base(p, s), half), :], bit)
         live[p].start()
-    for p in range(parts): launch(p, 0)
+
+    for p in range(count):
+        launch(p, 0)
     for s in range(stages):
-        for p in range(parts):
-            bit = orders[p][s]
+        for p in range(count):
+            side = side_of(parts[p][0][s])
             live[p].wait()
-            half = rows // 2 ** min(s + 1, stages - 1)
-            step = 16 if half % 64 else 64
-            got = recv[p].at[pl.ds(base[s], half), :]
+            half = size(p, s)
+            got = recv[p].at[pl.ds(base(p, s), half), :]
             if s == 0:
-                mine = side_of(bit) * half
-                whole[p] = mine
-                add_rows(acc[p], x_ref.at[:, columns[p]], got, 0, pl.multiple_of(mine, half), half, step)
-                start[p] = 0
+                place[p] = side * half
+                add_rows(acc[p], view(x_ref, p), got, 0, pl.multiple_of(side * half, half), half)
             elif s < stages - 1:
-                mine = pl.multiple_of(start[p] + side_of(bit) * half, half)
-                add_rows(acc[p], acc[p], got, mine, mine, half, step)
-                whole[p] = whole[p] + side_of(bit) * half
-                start[p] = start[p] + side_of(bit) * half
+                mine = pl.multiple_of(start[p] + side * half, half)
+                add_rows(acc[p], acc[p], got, mine, mine, half)
+                place[p] = place[p] + side * half
+                start[p] = start[p] + side * half
             else:
                 at = pl.multiple_of(start[p], half)
-                add_rows(out_ref.at[:, columns[p]], acc[p], got, pl.multiple_of(whole[p], half), at, half, step)
-            if s < stages - 1: launch(p, s + 1)
+                add_rows(view(out_ref, p), acc[p], got, pl.multiple_of(place[p], half), at, half)
+            if s < stages - 1:
+                launch(p, s + 1)
+
     def spread(p, s):
-        bit = orders[p][s]
-        half = rows // 2 ** (s + 1)
-        src = out_ref.at[pl.ds(pl.multiple_of(whole[p], half), half), columns[p]]
-        live[p] = copy(p, 2 * stages - 2 - s, src, src, bit)
+        half = size(p, s)
+        src = view(out_ref, p).at[pl.ds(pl.multiple_of(place[p], half), half), :]
+        live[p] = copy(p, 2 * stages - 2 - s, src, src, parts[p][0][s])
         live[p].start()
-    for p in range(parts): spread(p, stages - 2)
+
+    for p in range(count):
+        spread(p, stages - 2)
     for s in range(stages - 2, -1, -1):
-        for p in range(parts):
+        for p in range(count):
             live[p].wait()
-            whole[p] = whole[p] - side_of(orders[p][s]) * (rows // 2 ** (s + 1))
-            if s: spread(p, s - 1)
+            place[p] = place[p] - side_of(parts[p][0][s]) * size(p, s)
+            if s:
+                spread(p, s - 1)
+
 
 def total_of(x, dp, ring, collective_id):
     orders = bit_orders(dp, ring)
     rows, cols = x.shape
-    parts, stages = len(orders), len(orders[0])
-    wide = cols // parts
-    got = sum(rows // 2 ** min(s + 1, stages - 1) for s in range(stages))
+    stages = len(orders[0])
+    unit = 16 << (stages - 1)
+    first = -(-rows // unit // 2) * unit
+    spans = [(0, first), (first, rows - first)]
+    wide = cols // len(orders)
+    heights = [span[1] for span in spans for _ in orders]
     whole = pl.BlockSpec(memory_space=pltpu.VMEM)
-    return pl.pallas_call(functools.partial(sum_kernel, orders),
-        out_shape=jax.ShapeDtypeStruct(x.shape, BF), in_specs=[whole], out_specs=whole,
-        scratch_shapes=[pltpu.VMEM((rows // 2, wide), BF)] * parts + [pltpu.VMEM((got, wide), BF)] * parts
-        + [pltpu.SemaphoreType.DMA((parts, 2 * stages - 1))] * 2,
-        compiler_params=pltpu.CompilerParams(collective_id=collective_id, has_side_effects=True, vmem_limit_bytes=56*2**20),
-        name="total")(x)
+    return pl.pallas_call(
+        functools.partial(sum_kernel, orders, spans),
+        out_shape=jax.ShapeDtypeStruct(x.shape, BF),
+        in_specs=[whole],
+        out_specs=whole,
+        scratch_shapes=[pltpu.VMEM((h // 2, wide), BF) for h in heights]
+        + [
+            pltpu.VMEM((sum(h // 2 ** min(s + 1, stages - 1) for s in range(stages)), wide), BF)
+            for h in heights
+        ]
+        + [pltpu.SemaphoreType.DMA((len(heights), 2 * stages - 1))] * 2,
+        compiler_params=pltpu.CompilerParams(
+            collective_id=collective_id, has_side_effects=True, vmem_limit_bytes=40 * 2**20
+        ),
+        name="total",
+    )(x)
 
 
 def normal(h):

time: 351 us -> 342 us (0.974)
  Pallas kernels: 300 us -> 282 us
  waiting for transfers between devices: 0.07 us -> 12.4 us
    all_gather x1, waiting for transfers between devices: 0.02 us -> 12.4 us  [unpack(): everyone = lax.all_gather(parts, ('dp', 'seq'))]
    pallas_call x1, Pallas kernels: 79.9 us -> 68.8 us  [total_of(): pl.pallas_call(functools.partial(sum_kernel, orders, spans), out_shape=ja...]
    pallas_call x1, Pallas kernels: 155 us -> 146 us  [attention(): pl.pallas_call(functools.partial(attention_kernel, seqs, tiles // seqs, o...]
  transfers between devices with their start and end apart: 2 -> 2, of which waited for: 0 -> 1; matrix products, arithmetic and copies ran while one was open for 8% -> 7% of each run, Pallas kernels for 39% -> 37%
where the time goes in v1:
time: 342 us
  Pallas kernels  282 us (82%)
  between operations  14.6 us (4%)
  other arithmetic  14.4 us (4%)
  waiting for transfers between devices  12.4 us (4%)
  local copies, waits for them, and re-layouts  12.3 us (4%)
  matrix products  6.8 us (2%)
    pallas_call x1, Pallas kernels, attention(): pl.pallas_call(functools.partial(attention_kernel, seqs, tiles // seqs, o...  146 us
    pallas_call x1, Pallas kernels, total_of(): pl.pallas_call(functools.partial(sum_kernel, orders, spans), out_shape=ja...  68.8 us
    pallas_call x1, Pallas kernels, feed_forward(): pl.pallas_call(feed_kernel, grid=(steps,), out_shape=[jax.ShapeDtypeStruc...  41 us
    pallas_call x1, Pallas kernels, finish(): pl.pallas_call(finish_kernel, grid=(seqs,), out_shape=[jax.ShapeDtypeStru...  15.4 us
    all_gather x1, waiting for transfers between devices, unpack(): everyone = lax.all_gather(parts, ('dp', 'seq'))  12.4 us
    pallas_call x1, Pallas kernels, unpack(): pl.pallas_call(functools.partial(unpack_kernel, froms), out_shape=[jax.Sh...  10.2 us
  transfers between devices with their start and end apart: 2, of which 1 were waited for; matrix products, arithmetic and copies ran while one was open for 7% of the time, Pallas kernels for 37%

profile of v1, /device:TPU:0, one launch (start us, length us, event | category | flops | bytes accessed | tf_op | source)
XLA Modules:
  0.0 342.1 jit_solution(91566488354307451)
XLA Ops:
  7.2 0.0 copy-start.6
  7.2 0.0 copy-start.20
  7.2 0.0 copy-start.18
  7.2 0.0 copy-start.10
  7.3 0.0 copy-start.8
  7.3 0.0 all-gather.4.cloned.1.call-start
  7.3 0.8 convert_element_type.57
  8.1 1.7 convert_reduce_fusion
  9.8 2.0 fusion.8
  11.8 0.1 pad_maximum_fusion.2
  11.9 0.0 copy-start.7
  12.0 0.0 copy-start.23
  12.0 0.9 fusion.10
  12.9 0.2 subtract_convert_fusion
  13.1 0.7 pad_maximum_fusion.1
  13.9 0.0 all-gather.4.cloned.1.call-update
  13.9 0.0 all-gather.6.cloned.1.call-start
  14.0 3.3 add_bitcast_fusion
  17.3 3.5 %copy.45 = f32[4,768,256]{2,1,0:T(8,128)} copy(f32[4,768,256]{1,2,0:T(8,128)} %add_bitcast_fusion) | data formatting | bytes 6291456 | tf_op jit(solution)/shard_map/add | solution.py:1092
  20.8 1.8 slice.94
  22.7 1.2 multiply_subtract_fusion
  24.0 1.6 fusion.9
  25.5 1.8 fusion.7
  27.3 2.6 convolution_convert_fusion
  29.9 41.0 %feed_forward.1 = (f32[1024,768]{1,0:T(8,128)}, f32[1024,768]{1,0:T(8,128)}, bf16[3072,768]{1,0:T(8,128)(2,1)}, bf16[3072,768]{1,0:T(8,128)(2,1)}, f32[1,3072]{1,0:T(1,128)}) custom-call(bf16[1024,768]{1,0:T(8,128)(2,1)} %bitcast.43, bf16[1024,768]{1,0:T(8,128)(2,1)} %bitcast.46, bf16[768,3072]{1,0:T(8,128)(2,1)} %up_ref.1, bf16[3072,768]{1,0:T(8,128)(2,1)} %down_ref.1, ...), custom_call_target="tpu_custom_call" | custom-call | flops 28991029248 | bytes 37748736 | tf_op jit(solution)/shard_map/feed_forward/pallas_call | solution.py:116
  70.9 0.0 all-gather.4.cloned.1.call-done.all_ref
  70.9 0.0 copy-start.13
  70.9 0.0 copy-start.19
  70.9 0.0 copy-start.11
  70.9 0.0 copy-start.16
  71.0 146.2 %attention.1 = (bf16[16,192,256]{2,1,0:T(8,128)(2,1)}, bf16[16,192,256]{2,1,0:T(8,128)(2,1)}, bf16[4,8,256,128]{3,2,1,0:T(8,128)(2,1)}, bf16[2,96,768]{2,1,0:T(8,128)(2,1)}) custom-call(bf16[16,192,256]{2,1,0:T(8,128)(2,1)} %bitcast.44, bf16[16,192,256]{2,1,0:T(8,128)(2,1)} %bitcast.51, bf16[16,512,256]{2,1,0:T(8,128)(2,1)} %all-gather.4.cloned.1.call-done.all_ref, ...), custom_call_target="tpu_custom_call" | custom-call | flops 154618822656 | bytes 6291456 | tf_op jit(solution)/shard_map/attention/pallas_call | solution.py:706
  217.2 0.0 all-gather.6.cloned.1.call-update
  217.3 0.2 copy.46
  217.5 0.2 copy.47
  217.7 1.7 pad_maximum_fusion.weight_ref
  219.5 1.4 copy-done.4
  220.9 15.4 %finish.1 = (f32[1024,768]{1,0:T(8,128)}, f32[1024,768]{1,0:T(8,128)}, bf16[1792,768]{1,0:T(8,128)(2,1)}) custom-call(bf16[4,768,256]{2,1,0:T(8,128)(2,1)S(1)} %bitcast.37, bf16[4,768,256]{2,1,0:T(8,128)(2,1)S(1)} %bitcast.38, bf16[4,8,256,128]{3,2,1,0:T(8,128)(2,1)} %get-tuple-element.46.slot_ref, f32[4,8,256]{2,1,0:T(8,128)S(1)} %get-tuple-element.73.cos_ref, ...), custom_call_target="tpu_custom_call" | custom-call | flops 7247757312 | bytes 20447232 | tf_op jit(solution)/shard_map/finish/pallas_call | solution.py:1014
  236.3 0.0 copy-start
  236.3 1.8 copy-done
  238.0 68.8 %total.1 = bf16[1792,768]{1,0:T(8,128)(2,1)S(1)} custom-call(bf16[1792,768]{1,0:T(8,128)(2,1)S(1)} %copy-done), custom_call_target="tpu_custom_call" | custom-call | tf_op jit(solution)/shard_map/total/pallas_call | solution.py:886
  306.9 0.6 reshape.120
  307.5 0.6 slice_reduce_fusion
  308.1 0.6 slice_bitcast_fusion.2
  308.7 0.8 slice_bitcast_fusion
  309.5 2.5 slice_convert_fusion
  312.0 12.4 %all-gather.6.cloned.1.call-done = bf16[64,96,768]{2,1,0:T(8,128)(2,1)} async-done(((bf16[2,96,768]{2,1,0:T(8,128)(2,1)}), bf16[64,96,768]{2,1,0:T(8,128)(2,1)}) %all-gather.6.cloned.1.call-update) | async-done | bytes 9437200 | tf_op jit(solution)/shard_map/all_gather | solution.py:272
  324.4 10.2 %unpack.1 = (f32[3072,768]{1,0:T(8,128)}, f32[768,3072]{1,0:T(8,128)}) custom-call(bf16[32,2,96,768]{3,2,1,0:T(8,128)(2,1)} %bitcast.42), custom_call_target="tpu_custom_call" | custom-call | flops 9437184 | bytes 28311552 | tf_op jit(solution)/shard_map/unpack/pallas_call | solution.py:278
  334.7 0.6 copy.49
  (52 shorter events, 0.2 us)
Async XLA Ops:
  7.2 4.7 %copy-start.6 = (bf16[4,256,768]{2,1,0:T(8,128)(2,1)S(1)}, bf16[4,256,768]{2,1,0:T(8,128)(2,1)}, u32[]{:S(2)}) copy-start(bf16[4,256,768]{2,1,0:T(8,128)(2,1)} %param.19) | copy-start | bytes 4718596
  7.2 4.6 %copy-start.24 = (f32[64]{0:T(128)S(1)}, f32[64]{0:T(128)}, u32[]{:S(2)}) copy-start(f32[64]{0:T(128)} %param.30) | copy-start | bytes 772
  7.2 4.6 %copy-start.25 = (f32[64]{0:T(128)S(1)}, f32[64]{0:T(128)}, u32[]{:S(2)}) copy-start(f32[64]{0:T(128)} %param.28) | copy-start | bytes 772
  7.2 4.7 %copy-start.20 = (f32[768]{0:T(1024)S(1)}, f32[768]{0:T(1024)}, u32[]{:S(2)}) copy-start(f32[768]{0:T(1024)} %param.22) | copy-start | bytes 9220
  7.2 4.7 %copy-start.18 = (f32[768]{0:T(1024)S(1)}, f32[768]{0:T(1024)}, u32[]{:S(2)}) copy-start(f32[768]{0:T(1024)} %param.21) | copy-start | bytes 9220
  7.2 4.7 %copy-start.10 = (bf16[768,64]{0,1:T(8,128)(2,1)S(1)}, bf16[768,64]{0,1:T(8,128)(2,1)}, u32[]{:S(2)}) copy-start(bf16[768,64]{0,1:T(8,128)(2,1)} %param.29) | copy-start | bytes 294916
  7.3 4.7 %copy-start.8 = (bf16[768,64]{0,1:T(8,128)(2,1)S(1)}, bf16[768,64]{0,1:T(8,128)(2,1)}, u32[]{:S(2)}) copy-start(bf16[768,64]{0,1:T(8,128)(2,1)} %param.27) | copy-start | bytes 294916
  7.3 63.6 %all-gather.4.cloned.1.call-start = ((), (), s32[]{:S(2)}) async-start(), calls=%async_computation | async-start | bytes 4456448 | tf_op jit(solution)/shard_map/all_gather | solution.py:1090
  11.9 2.0 copy-start.7
  12.0 2.0 copy-start.23
  13.9 310.5 %all-gather.6.cloned.1.call-start = ((), (), s32[]{:S(2)}) async-start(), calls=%async_computation.1 | async-start | bytes 9732096 | tf_op jit(solution)/shard_map/all_gather | solution.py:272
  22.7 2.9 copy-start.12
  22.7 2.9 copy-start.15
  23.9 3.4 copy-start.1
  23.9 3.4 copy-start.22
  70.9 146.3 %copy-start.13 = (f32[768]{0:T(1024)S(1)}, f32[768]{0:T(1024)}, u32[]{:S(2)}) copy-start(f32[768]{0:T(1024)} %param.23) | copy-start | bytes 9220
  70.9 146.3 %copy-start.19 = (f32[768]{0:T(1024)S(1)}, f32[768]{0:T(1024)}, u32[]{:S(2)}) copy-start(f32[768]{0:T(1024)} %param.21) | copy-start | bytes 9220
  70.9 146.4 %copy-start.21 = (f32[768]{0:T(1024)S(1)}, f32[768]{0:T(1024)}, u32[]{:S(2)}) copy-start(f32[768]{0:T(1024)} %param.22) | copy-start | bytes 9220
  70.9 146.4 %copy-start.9 = (bf16[768,64]{0,1:T(8,128)(2,1)S(1)}, bf16[768,64]{0,1:T(8,128)(2,1)}, u32[]{:S(2)}) copy-start(bf16[768,64]{0,1:T(8,128)(2,1)} %param.27) | copy-start | bytes 294916
  70.9 146.5 %copy-start.11 = (bf16[768,64]{0,1:T(8,128)(2,1)S(1)}, bf16[768,64]{0,1:T(8,128)(2,1)}, u32[]{:S(2)}) copy-start(bf16[768,64]{0,1:T(8,128)(2,1)} %param.29) | copy-start | bytes 294916
  70.9 146.7 %copy-start.16 = (f32[768]{0:T(1024)S(1)}, f32[768]{0:T(1024)}, u32[]{:S(2)}) copy-start(f32[768]{0:T(1024)} %param.32) | copy-start | bytes 9220
  71.0 146.7 %copy-start.17 = (f32[768]{0:T(1024)S(1)}, f32[768]{0:T(1024)}, u32[]{:S(2)}) copy-start(f32[768]{0:T(1024)} %param.36) | copy-start | bytes 9220
  217.1 2.3 copy-start.2
  217.2 2.3 copy-start.3
  217.2 2.3 copy-start.5
  219.5 1.4 copy-start.4
  236.3 1.8 copy-start
  308.1 26.5 %copy-start.14 = (f32[768]{0:T(1024)}, f32[768]{0:T(1024)S(1)}, u32[]{:S(2)}) copy-start(f32[768]{0:T(1024)S(1)} %get-tuple-element.109) | copy-start | bytes 9220
Sparse Core Ops, SparseCore 0:
  14.0 53.2 all-gather.3
  217.3 107.0 all-gather.5

commit v2 on v1

--- a/solution.py
+++ b/solution.py
@@ -640,6 +640,7 @@
             return c
 
         lax.fori_loop(0, length // KEYS, turn, 0)
+        pl.when(s + 1 < seqs)(lambda: start_in(s + 1))
         given = given_of(s)
         own = groups - upper * given
         taken = (1 - upper) * given
@@ -654,7 +655,6 @@
             position = jnp.where(mine, me, partner)
             state = tile(mine, t, k, position, acted, progress)
             pl.when((u == 0) & (s > 0))(lambda: pass_on(s - 1))
-            pl.when((u == 0) & (s + 1 < seqs))(lambda: start_in(s + 1))
             return state
 
         state = lax.fori_loop(0, own + taken, work, state)

time: 342 us -> 340 us (level)
  transfers between devices with their start and end apart: 2 -> 2, of which waited for: 1 -> 1; matrix products, arithmetic and copies ran while one was open for 7% -> 7% of each run, Pallas kernels for 37% -> 36%
where the time goes in v2:
time: 340 us
  Pallas kernels  280 us (82%)
  between operations  14.6 us (4%)
  other arithmetic  14.4 us (4%)
  local copies, waits for them, and re-layouts  12.3 us (4%)
  waiting for transfers between devices  11.9 us (4%)
  matrix products  6.8 us (2%)
    pallas_call x1, Pallas kernels, attention(): pl.pallas_call(functools.partial(attention_kernel, seqs, tiles // seqs, o...  146 us
    pallas_call x1, Pallas kernels, total_of(): pl.pallas_call(functools.partial(sum_kernel, orders, spans), out_shape=ja...  67.5 us
    pallas_call x1, Pallas kernels, feed_forward(): pl.pallas_call(feed_kernel, grid=(steps,), out_shape=[jax.ShapeDtypeStruc...  41 us
    pallas_call x1, Pallas kernels, finish(): pl.pallas_call(finish_kernel, grid=(seqs,), out_shape=[jax.ShapeDtypeStru...  15.4 us
    all_gather x1, waiting for transfers between devices, unpack(): everyone = lax.all_gather(parts, ('dp', 'seq'))  11.9 us
    pallas_call x1, Pallas kernels, unpack(): pl.pallas_call(functools.partial(unpack_kernel, froms), out_shape=[jax.Sh...  10.2 us
  transfers between devices with their start and end apart: 2, of which 1 were waited for; matrix products, arithmetic and copies ran while one was open for 7% of the time, Pallas kernels for 36%

profile of v2, /device:TPU:0, one launch (start us, length us, event | category | flops | bytes accessed | tf_op | source)
XLA Modules:
  0.0 340.1 jit_solution(16302290767141430377)
XLA Ops:
  7.2 0.0 copy-start.20
  7.2 0.0 copy-start.18
  7.3 0.0 copy-start.8
  7.3 0.0 all-gather.4.cloned.1.call-start
  7.3 0.8 convert_element_type.57
  8.1 1.7 convert_reduce_fusion
  9.8 2.0 fusion.8
  11.8 0.1 pad_maximum_fusion.2
  12.0 0.0 copy-start.23
  12.0 0.9 fusion.10
  12.9 0.2 subtract_convert_fusion
  13.1 0.7 pad_maximum_fusion.1
  13.9 0.0 all-gather.4.cloned.1.call-update
  13.9 0.0 all-gather.6.cloned.1.call-start
  14.0 3.3 add_bitcast_fusion
  17.3 3.5 %copy.45 = f32[4,768,256]{2,1,0:T(8,128)} copy(f32[4,768,256]{1,2,0:T(8,128)} %add_bitcast_fusion) | data formatting | bytes 6291456 | tf_op jit(solution)/shard_map/add | solution.py:1092
  20.8 1.8 slice.94
  22.7 0.0 copy-start.12
  22.7 0.0 copy-start.15
  22.7 1.2 multiply_subtract_fusion
  23.9 0.0 copy-start.1
  23.9 0.0 copy-start.22
  24.0 1.6 fusion.9
  25.5 1.8 fusion.7
  27.3 2.6 convolution_convert_fusion
  29.9 41.0 %feed_forward.1 = (f32[1024,768]{1,0:T(8,128)}, f32[1024,768]{1,0:T(8,128)}, bf16[3072,768]{1,0:T(8,128)(2,1)}, bf16[3072,768]{1,0:T(8,128)(2,1)}, f32[1,3072]{1,0:T(1,128)}) custom-call(bf16[1024,768]{1,0:T(8,128)(2,1)} %bitcast.43, bf16[1024,768]{1,0:T(8,128)(2,1)} %bitcast.46, bf16[768,3072]{1,0:T(8,128)(2,1)} %up_ref.1, bf16[3072,768]{1,0:T(8,128)(2,1)} %down_ref.1, ...), custom_call_target="tpu_custom_call" | custom-call | flops 28991029248 | bytes 37748736 | tf_op jit(solution)/shard_map/feed_forward/pallas_call | solution.py:116
  70.9 0.0 all-gather.4.cloned.1.call-done.all_ref
  70.9 0.0 copy-start.21
  70.9 0.0 copy-start.9
  71.0 0.0 copy-start.17
  71.0 146.0 %attention.1 = (bf16[16,192,256]{2,1,0:T(8,128)(2,1)}, bf16[16,192,256]{2,1,0:T(8,128)(2,1)}, bf16[4,8,256,128]{3,2,1,0:T(8,128)(2,1)}, bf16[2,96,768]{2,1,0:T(8,128)(2,1)}) custom-call(bf16[16,192,256]{2,1,0:T(8,128)(2,1)} %bitcast.44, bf16[16,192,256]{2,1,0:T(8,128)(2,1)} %bitcast.51, bf16[16,512,256]{2,1,0:T(8,128)(2,1)} %all-gather.4.cloned.1.call-done.all_ref, ...), custom_call_target="tpu_custom_call" | custom-call | flops 154618822656 | bytes 6291456 | tf_op jit(solution)/shard_map/attention/pallas_call | solution.py:706
  216.9 0.0 copy-start.2
  217.0 0.0 all-gather.6.cloned.1.call-update
  217.1 0.2 copy.46
  217.3 0.2 copy.47
  217.5 1.7 pad_maximum_fusion.weight_ref
  219.3 1.4 copy-done.4
  220.7 15.4 %finish.1 = (f32[1024,768]{1,0:T(8,128)}, f32[1024,768]{1,0:T(8,128)}, bf16[1792,768]{1,0:T(8,128)(2,1)}) custom-call(bf16[4,768,256]{2,1,0:T(8,128)(2,1)S(1)} %bitcast.37, bf16[4,768,256]{2,1,0:T(8,128)(2,1)S(1)} %bitcast.38, bf16[4,8,256,128]{3,2,1,0:T(8,128)(2,1)} %get-tuple-element.46.slot_ref, f32[4,8,256]{2,1,0:T(8,128)S(1)} %get-tuple-element.73.cos_ref, ...), custom_call_target="tpu_custom_call" | custom-call | flops 7247757312 | bytes 20447232 | tf_op jit(solution)/shard_map/finish/pallas_call | solution.py:1014
  236.1 1.8 copy-done
  237.8 67.5 %total.1 = bf16[1792,768]{1,0:T(8,128)(2,1)S(1)} custom-call(bf16[1792,768]{1,0:T(8,128)(2,1)S(1)} %copy-done), custom_call_target="tpu_custom_call" | custom-call | tf_op jit(solution)/shard_map/total/pallas_call | solution.py:886
  305.4 0.6 reshape.120
  306.0 0.6 slice_reduce_fusion
  306.7 0.6 slice_bitcast_fusion.2
  307.3 0.8 slice_bitcast_fusion
  308.0 2.5 slice_convert_fusion
  310.6 11.9 %all-gather.6.cloned.1.call-done = bf16[64,96,768]{2,1,0:T(8,128)(2,1)} async-done(((bf16[2,96,768]{2,1,0:T(8,128)(2,1)}), bf16[64,96,768]{2,1,0:T(8,128)(2,1)}) %all-gather.6.cloned.1.call-update) | async-done | bytes 9437200 | tf_op jit(solution)/shard_map/all_gather | solution.py:272
  322.5 10.2 %unpack.1 = (f32[3072,768]{1,0:T(8,128)}, f32[768,3072]{1,0:T(8,128)}) custom-call(bf16[32,2,96,768]{3,2,1,0:T(8,128)(2,1)} %bitcast.42), custom_call_target="tpu_custom_call" | custom-call | flops 9437184 | bytes 28311552 | tf_op jit(solution)/shard_map/unpack/pallas_call | solution.py:278
  332.7 0.6 copy.49
  (52 shorter events, 0.2 us)
Async XLA Ops:
  7.2 4.7 %copy-start.6 = (bf16[4,256,768]{2,1,0:T(8,128)(2,1)S(1)}, bf16[4,256,768]{2,1,0:T(8,128)(2,1)}, u32[]{:S(2)}) copy-start(bf16[4,256,768]{2,1,0:T(8,128)(2,1)} %param.19) | copy-start | bytes 4718596
  7.2 4.6 %copy-start.24 = (f32[64]{0:T(128)S(1)}, f32[64]{0:T(128)}, u32[]{:S(2)}) copy-start(f32[64]{0:T(128)} %param.30) | copy-start | bytes 772
  7.2 4.6 %copy-start.25 = (f32[64]{0:T(128)S(1)}, f32[64]{0:T(128)}, u32[]{:S(2)}) copy-start(f32[64]{0:T(128)} %param.28) | copy-start | bytes 772
  7.2 4.7 %copy-start.20 = (f32[768]{0:T(1024)S(1)}, f32[768]{0:T(1024)}, u32[]{:S(2)}) copy-start(f32[768]{0:T(1024)} %param.22) | copy-start | bytes 9220
  7.2 4.7 %copy-start.18 = (f32[768]{0:T(1024)S(1)}, f32[768]{0:T(1024)}, u32[]{:S(2)}) copy-start(f32[768]{0:T(1024)} %param.21) | copy-start | bytes 9220
  7.2 4.7 %copy-start.10 = (bf16[768,64]{0,1:T(8,128)(2,1)S(1)}, bf16[768,64]{0,1:T(8,128)(2,1)}, u32[]{:S(2)}) copy-start(bf16[768,64]{0,1:T(8,128)(2,1)} %param.29) | copy-start | bytes 294916
  7.3 4.7 %copy-start.8 = (bf16[768,64]{0,1:T(8,128)(2,1)S(1)}, bf16[768,64]{0,1:T(8,128)(2,1)}, u32[]{:S(2)}) copy-start(bf16[768,64]{0,1:T(8,128)(2,1)} %param.27) | copy-start | bytes 294916
  7.3 63.6 %all-gather.4.cloned.1.call-start = ((), (), s32[]{:S(2)}) async-start(), calls=%async_computation | async-start | bytes 4456448 | tf_op jit(solution)/shard_map/all_gather | solution.py:1090
  11.9 2.0 copy-start.7
  12.0 2.0 copy-start.23
  13.9 308.6 %all-gather.6.cloned.1.call-start = ((), (), s32[]{:S(2)}) async-start(), calls=%async_computation.1 | async-start | bytes 9732096 | tf_op jit(solution)/shard_map/all_gather | solution.py:272
  22.7 2.9 copy-start.12
  22.7 2.9 copy-start.15
  23.9 3.4 copy-start.1
  23.9 3.4 copy-start.22
  70.9 146.1 %copy-start.13 = (f32[768]{0:T(1024)S(1)}, f32[768]{0:T(1024)}, u32[]{:S(2)}) copy-start(f32[768]{0:T(1024)} %param.23) | copy-start | bytes 9220
  70.9 146.1 %copy-start.19 = (f32[768]{0:T(1024)S(1)}, f32[768]{0:T(1024)}, u32[]{:S(2)}) copy-start(f32[768]{0:T(1024)} %param.21) | copy-start | bytes 9220
  70.9 146.1 %copy-start.21 = (f32[768]{0:T(1024)S(1)}, f32[768]{0:T(1024)}, u32[]{:S(2)}) copy-start(f32[768]{0:T(1024)} %param.22) | copy-start | bytes 9220
  70.9 146.2 %copy-start.9 = (bf16[768,64]{0,1:T(8,128)(2,1)S(1)}, bf16[768,64]{0,1:T(8,128)(2,1)}, u32[]{:S(2)}) copy-start(bf16[768,64]{0,1:T(8,128)(2,1)} %param.27) | copy-start | bytes 294916
  70.9 146.3 %copy-start.11 = (bf16[768,64]{0,1:T(8,128)(2,1)S(1)}, bf16[768,64]{0,1:T(8,128)(2,1)}, u32[]{:S(2)}) copy-start(bf16[768,64]{0,1:T(8,128)(2,1)} %param.29) | copy-start | bytes 294916
  70.9 146.5 %copy-start.16 = (f32[768]{0:T(1024)S(1)}, f32[768]{0:T(1024)}, u32[]{:S(2)}) copy-start(f32[768]{0:T(1024)} %param.32) | copy-start | bytes 9220
  71.0 146.5 %copy-start.17 = (f32[768]{0:T(1024)S(1)}, f32[768]{0:T(1024)}, u32[]{:S(2)}) copy-start(f32[768]{0:T(1024)} %param.36) | copy-start | bytes 9220
  216.9 2.3 copy-start.2
  216.9 2.3 copy-start.3
  217.0 2.3 copy-start.5
  219.3 1.4 copy-start.4
  236.0 1.8 copy-start
  306.7 26.0 %copy-start.14 = (f32[768]{0:T(1024)}, f32[768]{0:T(1024)S(1)}, u32[]{:S(2)}) copy-start(f32[768]{0:T(1024)S(1)} %get-tuple-element.109) | copy-start | bytes 9220
Sparse Core Ops, SparseCore 0:
  14.0 53.2 all-gather.3
  217.1 105.2 all-gather.5
